TPU v7x, 32 devices: a whole 2x2x4 slice. The times are simulated.
32 devices in a mesh: groups: 2 (over y), tile: 16 (over z, x, core).
Axes of the slice: x: 2, y: 2, z: 4, core: 2. Of those that a mesh axis runs over, the one named last changes fastest.
Arguments:
- object_slices: float32 [4096, 2, 2, 256], P(('groups', 'tile')), parts along dimension 0, may hold values from -4 to 4
- probe_field: float32 [256, 2, 2, 128], P(('groups', 'tile')), parts along dimension 0, may hold values from -2.5 to 2.5
- patterns: float32 [512, 128, 128], P(('groups', 'tile')), parts along dimension 0, may hold values from 0 to 2
- row_offsets: int32 [512], P(('groups', 'tile')), parts along dimension 0, may hold values from 0 to 127
- col_offsets: int32 [512], P(('groups', 'tile')), parts along dimension 0, may hold values from 0 to 128
- counts: int32 [32], P(('groups', 'tile')), parts along dimension 0, may hold values from 1 to 16, as said below
Outputs:
- object_grad: float32 [4096, 2, 2, 256], P(('groups', 'tile')), parts along dimension 0
- probe_grad: float32 [256, 2, 2, 128], P(('groups', 'tile')), parts along dimension 0
There are 2 independent parts, one for each index of `groups`. A program takes and returns all parts, laid end to end along the dimension named above; each array names one. Nothing has to cross between parts.
Inputs may be any that keep to these rules, and one draw needn't show every extreme that they name: `counts`: each tile has 1 to 16 live slots, and one tile of every draw has 16.
All inputs are finite; a program needn't handle non-finite values.
Results may differ from a plain program's by a relative error of at most 0.0003.
Values sent between devices are 32-bit elements; how exact they have to be, the bound alone decides.
No kernel may reach another device: no remote copies, remote signals or barrier semaphores. Data moves between devices by JAX's collectives and lax.ppermute only.
A program may use at most 64 MiB of HBM per device.

v0:
```python
import math

import jax
import jax.numpy as jnp
import numpy as np
from jax import lax
from jax.experimental import pallas as pl
from jax.experimental.pallas import tpu as pltpu
from jax.sharding import PartitionSpec as P

GROUP_DEV = 16
KAPPA = 4.0
MODES = 2
SLICES = 2
HALVES = 2
AHEAD = (0, 8, 4, 12, 2, 10, 6, 14)


def factors(extent):
    counter = np.arange(extent)
    half = extent // 2
    dft = np.exp(-2j * np.pi * (counter[:, None] * counter[None, :] % extent) / extent) / math.sqrt(extent)
    freq = ((counter + extent // 2) % extent - extent // 2) / extent
    prop = np.conj(dft) @ (np.exp(-1j * np.pi * KAPPA * freq**2)[:, None] * dft)
    whole = [part for matrix in (dft, prop) for part in (matrix.real, matrix.imag)]
    same, cross = prop[:half, :half], prop[:half, half:]
    even, odd = dft[0::2, :half], dft[1::2, :half]
    halves = [even, odd, np.conj(even.T), np.conj(odd.T),
              (same + cross) / 2, (same - cross) / 2, np.conj(same + cross) / 2, np.conj(same - cross) / 2]
    halves = [np.block([[m.real, -m.imag], [m.imag, m.real]]) for m in halves]
    return np.stack(whole + halves).astype(np.float32)


def split(value):
    high = value.astype(jnp.bfloat16)
    low = (value - high.astype(jnp.float32)).astype(jnp.bfloat16)
    return high, low


def prepare(own_ref, patterns_ref, factors_ref, planes_out, patterns_out, mats_out, half_out, own, parts, sems):
    copies = [pltpu.make_async_copy(source, target, sems.at[i]) for i, (source, target) in enumerate(
        ((factors_ref, parts), (own_ref, own), (patterns_ref, patterns_out)))]
    for copy in copies:
        copy.start()
    copies[0].wait()
    extent = parts.shape[1]
    for kind in range(2):
        real, imag = split(parts[2 * kind]), split(parts[2 * kind + 1])
        for conj in range(2):
            for k in range(2):
                mat = 4 * kind + 2 * conj + k
                upper, lower = (-imag[k], imag[k]) if conj else (imag[k], -imag[k])
                mats_out[mat, :extent, :extent] = real[k]
                mats_out[mat, :extent, extent:] = upper
                mats_out[mat, extent:, :extent] = lower
                mats_out[mat, extent:, extent:] = real[k]
    for k in range(half_out.shape[0]):
        high, low = split(parts[4 + k])
        half_out[k, :extent, :extent] = high
        half_out[k, :extent, extent:] = high
        half_out[k, extent:, :extent] = low
        half_out[k, extent:, extent:] = low
    copies[1].wait()
    rows = planes_out.shape[1]
    for layer in range(SLICES):
        for half in range(HALVES):
            for part in range(2):
                source = (layer * HALVES + half) * 2 + part
                plane = (layer * 2 + part) * HALVES + half
                planes_out[plane] = own[pl.ds(source, rows, stride=8), :]
    copies[2].wait()


def times(a, b):
    return [a[0] * b[0] - a[1] * b[1], a[0] * b[1] + a[1] * b[0]]


def conj_times(a, b):
    return [a[0] * b[0] + a[1] * b[1], a[0] * b[1] - a[1] * b[0]]


def add(a, b):
    return [a[0] + b[0], a[1] + b[1]]


def member_rows(member, order, share):
    return pl.ds(pl.multiple_of(lax.bitwise_xor(member, order) * share, share), share)


def place(probe_ref, keep_out, send_out):
    lanes, extent = probe_ref.shape[:2]
    share = extent // GROUP_DEV
    member = lax.rem(lax.axis_index("tile"), GROUP_DEV)
    for odd, ref in enumerate((keep_out, send_out)):
        for block in range(GROUP_DEV // 2):
            there = lax.bitwise_xor(lax.rem(member + block // 2 * 4, GROUP_DEV), 2 * (block % 2) + odd)
            for k in range(lanes):
                rows = pl.ds(block * share * lanes + k, share, stride=lanes)
                ref[rows, :] = probe_ref[k, pl.ds(pl.multiple_of(there * share, share), share), :]


def kernel(scalars_ref, own_ref, low_ref, high_ref, near_ref, far_ref, patterns_ref, mats_ref,
           half_ref, own_out, next_out, probe_acc, obj, acc, probe):
    most, extent = patterns_ref.shape[:2]
    share = extent // GROUP_DEV
    member = lax.rem(lax.axis_index("tile"), GROUP_DEV)
    tile_rows = own_ref.shape[1]
    middle = extent // 2
    lanes = 2 * MODES
    modes = range(MODES)

    for layer in range(SLICES):
        for half in range(HALVES):
            for part in range(2):
                source = (layer * HALVES + half) * 2 + part
                plane = (layer * 2 + part) * HALVES + half
                obj[plane, :tile_rows] = own_ref[plane]
                obj[plane, tile_rows:tile_rows + middle] = low_ref[pl.ds(source, middle, stride=8), :]
                obj[plane, tile_rows + middle:] = high_ref[pl.ds(source, extent - middle, stride=8), :]
    for odd, ref in enumerate((near_ref, far_ref)):
        for block, order in enumerate(AHEAD):
            for k in range(lanes):
                rows = pl.ds(block * share * lanes + k, share, stride=lanes)
                probe[k, member_rows(member, order + odd, share), :] = ref[rows, :]
    acc[...] = jnp.zeros(acc.shape, jnp.float32)
    probe_acc[...] = jnp.zeros(probe_acc.shape, jnp.float32)

    def right(fields, kind, conj):
        high_m, low_m = mats_ref[4 * kind + 2 * conj], mats_ref[4 * kind + 2 * conj + 1]
        rows = jnp.concatenate([jnp.concatenate(f[m], axis=1) for f in fields for m in modes], axis=0)
        high, low = split(rows)
        out = jnp.dot(jnp.concatenate([high, low, high], axis=1), jnp.concatenate([high_m, high_m, low_m], axis=0),
                      preferred_element_type=jnp.float32)
        return [[[out[(i * MODES + m) * extent:(i * MODES + m + 1) * extent, c * extent:(c + 1) * extent]
                  for c in range(2)] for m in modes] for i in range(len(fields))]

    def left(fields, kind, conj):
        middle = extent // 2
        cols = [jnp.concatenate([f[m][c] for f in fields for m in modes], axis=1) for c in range(2)]
        upper, lower = [c[:middle] for c in cols], [c[middle:] for c in cols]
        if kind == 1 or not conj:
            upper, lower = add(upper, lower), [u - v for u, v in zip(upper, lower)]
        halves = []
        for k, pieces in enumerate((upper, lower)):
            high, low = split(jnp.concatenate(pieces, axis=0))
            out = jnp.dot(half_ref[4 * kind + 2 * conj + k], jnp.concatenate([high, low], axis=0),
                          preferred_element_type=jnp.float32)
            out = out[:extent] + out[extent:]
            halves.append([out[:middle], out[middle:]])
        upper, lower = halves
        if kind == 1 or conj:
            upper, lower = add(upper, lower), [u - v for u, v in zip(upper, lower)]
        out = [jnp.concatenate([upper[c], lower[c]], axis=0) for c in range(2)]
        return [[[out[c][:, (i * MODES + m) * extent:(i * MODES + m + 1) * extent] for c in range(2)]
                 for m in modes] for i in range(len(fields))]

    lane = lax.broadcasted_iota(jnp.int32, (extent, extent), 1)

    def window(slot):
        r, c = scalars_ref[slot], scalars_ref[most + slot]
        shift = lax.rem(extent - c, extent)
        layers = []
        for layer in range(SLICES):
            parts = []
            for part in range(2):
                plane = (layer * 2 + part) * HALVES
                joined = jnp.where(lane >= c, obj[plane, pl.ds(r, extent), :], obj[plane + 1, pl.ds(r, extent), :])
                parts.append(pltpu.roll(joined, shift, 1))
            layers.append(parts)
        return layers

    def deposit(slot, layer, grad):
        r, c = scalars_ref[slot], scalars_ref[most + slot]
        for part in range(2):
            plane = (layer * 2 + part) * HALVES
            rolled = pltpu.roll(grad[part], lax.rem(c, extent), 1)
            acc[plane, pl.ds(r, extent), :] += jnp.where(lane >= c, rolled, 0.0)
            acc[plane + 1, pl.ds(r, extent), :] += jnp.where(lane >= c, 0.0, rolled)

    def measured(slot):
        return jnp.concatenate([patterns_ref[slot, pl.ds(k, extent // 2, stride=2), :] for k in range(2)], axis=0)

    def steps(slots):
        n = range(len(slots))
        field = [[probe[2 * m], probe[2 * m + 1]] for m in modes]
        objects = [window(slot) for slot in slots]
        state = right([[times(field[m], objects[i][0]) for m in modes] for i in n], 1, 0)
        yield
        entering = left(state, 1, 0)
        yield
        state = right([[times(entering[i][m], objects[i][1]) for m in modes] for i in n], 0, 0)
        yield
        state = left(state, 0, 0)
        yield
        weight = [2.0 * (sum(state[i][m][c] * state[i][m][c] for m in modes for c in range(2)) - measured(slots[i]))
                  for i in n]
        state = right([[[weight[i] * state[i][m][c] for c in range(2)] for m in modes] for i in n], 0, 1)
        yield
        state = left(state, 0, 1)
        yield
        for i in n:
            grad = conj_times(entering[i][0], state[i][0])
            for m in modes[1:]:
                grad = add(grad, conj_times(entering[i][m], state[i][m]))
            deposit(slots[i], 1, grad)
        state = right([[conj_times(objects[i][1], state[i][m]) for m in modes] for i in n], 1, 1)
        yield
        state = left(state, 1, 1)
        yield
        for i in n:
            grad = conj_times(field[0], state[i][0])
            for m in modes[1:]:
                grad = add(grad, conj_times(field[m], state[i][m]))
            deposit(slots[i], 0, grad)
        for m in modes:
            term = conj_times(objects[0][0], state[0][m])
            for i in n[1:]:
                term = add(term, conj_times(objects[i][0], state[i][m]))
            probe_acc[2 * m] += term[0]
            probe_acc[2 * m + 1] += term[1]

    def run(*sets):
        running = [steps(slots) for slots in sets]
        while running:
            running = [r for r in running if next(r, "done") is None]

    count = scalars_ref[2 * most]
    fours = lax.shift_right_logical(count, 2)

    def four(j, carry):
        run([4 * j, 4 * j + 1], [4 * j + 2, 4 * j + 3])
        return carry

    lax.fori_loop(0, fours, four, 0)

    @pl.when(lax.bitwise_and(count, 2) == 2)
    def _():
        run([4 * fours], [4 * fours + 1])

    @pl.when(lax.bitwise_and(count, 1) == 1)
    def _():
        run([count - 1])

    for layer in range(SLICES):
        for half in range(HALVES):
            for part in range(2):
                target = (layer * HALVES + half) * 2 + part
                plane = (layer * 2 + part) * HALVES + half
                own_out[pl.ds(target, tile_rows, stride=8), :] = acc[plane, :tile_rows]
                next_out[pl.ds(target, extent, stride=8), :] = acc[plane, tile_rows:]


def prepared(own, patterns):
    extent = patterns.shape[1]
    vmem = pl.BlockSpec(memory_space=pltpu.VMEM)
    parts = jnp.asarray(factors(extent))
    return pl.pallas_call(
        prepare,
        out_shape=(
            jax.ShapeDtypeStruct((8, own.shape[0] // 8, own.shape[1]), jnp.float32),
            jax.ShapeDtypeStruct(patterns.shape, jnp.float32),
            jax.ShapeDtypeStruct((8, 2 * extent, 2 * extent), jnp.bfloat16),
            jax.ShapeDtypeStruct((8, 2 * extent, 2 * extent), jnp.bfloat16),
        ),
        in_specs=[pl.BlockSpec(memory_space=pltpu.HBM)] * 3,
        out_specs=(vmem,) * 4,
        scratch_shapes=[
            pltpu.VMEM(own.shape, jnp.float32),
            pltpu.VMEM(parts.shape, jnp.float32),
            pltpu.SemaphoreType.DMA((3,)),
        ],
        compiler_params=pltpu.CompilerParams(vmem_limit_bytes=16 * 1024 * 1024),
        cost_estimate=pl.CostEstimate(flops=0, bytes_accessed=6 * 1024 * 1024, transcendentals=0),
    )(own, patterns, parts)


def terms(scalars, planes, low, high, near, far, patterns, mats):
    extent = patterns.shape[1]
    rows = planes.shape[1] + extent
    smem = pl.BlockSpec(memory_space=pltpu.SMEM)
    vmem = pl.BlockSpec(memory_space=pltpu.VMEM)
    return pl.pallas_call(
        kernel,
        out_shape=(
            jax.ShapeDtypeStruct((planes.shape[1] * 8, extent), jnp.float32),
            jax.ShapeDtypeStruct((extent * 8, extent), jnp.float32),
            jax.ShapeDtypeStruct((2 * MODES, extent, extent), jnp.float32),
        ),
        in_specs=[smem] + [vmem] * 8,
        out_specs=(vmem,) * 3,
        scratch_shapes=[
            pltpu.VMEM((8, rows, extent), jnp.float32),
            pltpu.VMEM((8, rows, extent), jnp.float32),
            pltpu.VMEM((2 * MODES, extent, extent), jnp.float32),
        ],
        compiler_params=pltpu.CompilerParams(vmem_limit_bytes=40 * 1024 * 1024),
    )(scalars, planes, low, high, near, far, patterns, *mats)


def placed(probe_grad, shape):
    vmem = pl.BlockSpec(memory_space=pltpu.VMEM)
    return pl.pallas_call(
        place,
        out_shape=(jax.ShapeDtypeStruct(shape, jnp.float32),) * 2,
        in_specs=[vmem],
        out_specs=(vmem,) * 2,
        compiler_params=pltpu.CompilerParams(vmem_limit_bytes=4 * 1024 * 1024),
    )(probe_grad)


def flat(block):
    rows, k, parts, columns = block.shape
    split_up = block.reshape(rows, k, parts, columns // 128, 128)
    return split_up.transpose(0, 1, 3, 2, 4).reshape(-1, 128)


def unflat(value, shape):
    rows, k, parts, columns = shape
    return value.reshape(rows, k, columns // 128, parts, 128).transpose(0, 1, 3, 2, 4).reshape(shape)


def partner(value, bits):
    return lax.ppermute(value, "tile", [(i, i ^ bits) for i in range(lax.axis_size("tile"))])


def halved(value):
    return value[:value.shape[0] // 2], value[value.shape[0] // 2:]


def places_on(value, distance):
    members = range(lax.axis_size("tile"))
    return lax.ppermute(value, "tile", [
        (i, i // GROUP_DEV * GROUP_DEV + (i + distance) % GROUP_DEV) for i in members])


def probe_share(probe_grad, shape):
    keep, send = placed(probe_grad, shape)
    blocks = jnp.split(keep + partner(send, 1), 4, axis=0)
    total = blocks[0] + sum(places_on(block, 4 * k) for k, block in enumerate(blocks) if k > 0)
    keep, send = halved(total)
    return keep + partner(send, 2)


def shards(object_slices, probe_field, patterns, row_offsets, col_offsets, counts):
    size = lax.axis_size("tile")
    down = [((i + 1) % size, i) for i in range(size)]
    own = flat(object_slices)
    low, high = halved(own)
    scalars = jnp.concatenate([row_offsets, col_offsets, counts])

    low = lax.ppermute(low, "tile", down)
    mine = flat(probe_field)
    quarter = mine
    for bits in (8, 4):
        quarter = jnp.concatenate([quarter, partner(quarter, bits)], axis=0)
    high, quarter, patterns, own = lax.optimization_barrier((high, quarter, patterns, own))
    near = jnp.concatenate([quarter, partner(quarter, 2)], axis=0)
    high = lax.ppermute(high, "tile", down)
    planes, patterns, *mats = prepared(own, patterns)
    near, planes, patterns, scalars, *mats = lax.optimization_barrier((near, planes, patterns, scalars, *mats))
    far = partner(near, 1)

    own_grad, back, probe_grad = terms(scalars, planes, low, high, near, far, patterns, mats)

    back = lax.ppermute(back, "tile", [(i, (i + 1) % size) for i in range(size)])
    probe_sum = lax.cond(
        counts[0] > 0,
        lambda grad: probe_share(grad, near.shape),
        lambda grad: jnp.zeros((near.shape[0] // 8, near.shape[1]), jnp.float32),
        probe_grad)
    object_grad = own_grad + back
    return unflat(object_grad, object_slices.shape), unflat(probe_sum, probe_field.shape)


def solution(mesh):
    in_specs = (
        P(("groups", "tile"), None, None, None),
        P(("groups", "tile"), None, None, None),
        P(("groups", "tile"), None, None),
        P(("groups", "tile")),
        P(("groups", "tile")),
        P(("groups", "tile")),
    )
    out_specs = (P(("groups", "tile"), None, None, None), P(("groups", "tile"), None, None, None))
    return jax.shard_map(shards, mesh=mesh, in_specs=in_specs, out_specs=out_specs, check_vma=False)
```

profile of v0, /device:TPU:0, one launch (start us, length us, event | category | flops | bytes accessed | tf_op | source)
XLA Modules:
  0.0 54.7 jit_solution(5048657413362523659)
XLA Ops:
  0.6 4.1 %collective-permute-start.5 = (f32[32,128]{1,0:T(8,128)}, f32[32,128]{1,0:T(8,128)S(1)}, u32[]{:S(2)}, u32[]{:S(2)}) collective-permute-start(f32[32,128]{1,0:T(8,128)} %bitcast.20), channel_id=1, source_target_pairs={{0,8},{1,9},{2,10},{3,11},{4,12},{5,13},{6,14},{7,15},{8,0},{9,1},... | collective-permute-start | bytes 49160 | tf_op jit(solution)/shard_map/ppermute | solution.py:323
  4.7 1.9 %collective-permute-done.5 = f32[32,128]{1,0:T(8,128)S(1)} collective-permute-done((f32[32,128]{1,0:T(8,128)}, f32[32,128]{1,0:T(8,128)S(1)}, u32[]{:S(2)}, u32[]{:S(2)}) %collective-permute-start.5) | collective-permute-done | bytes 16416 | tf_op jit(solution)/shard_map/ppermute | solution.py:323
  6.7 0.7 %pad_maximum_fusion.2 = f32[64,128]{1,0:T(8,128)S(1)} fusion(f32[32,128]{1,0:T(8,128)S(1)} %collective-permute-done.5, f32[32,128]{1,0:T(8,128)} %bitcast.21), kind=kLoop, calls=%fused_computation.4 | loop fusion | flops 8192 | bytes 65536 | tf_op jit(solution)/shard_map/concatenate | solution.py:355
  7.4 1.9 %collective-permute-start.6 = (f32[64,128]{1,0:T(8,128)S(1)}, f32[64,128]{1,0:T(8,128)S(1)}, u32[]{:S(2)}, u32[]{:S(2)}) collective-permute-start(f32[64,128]{1,0:T(8,128)S(1)} %pad_maximum_fusion.2), channel_id=1, source_target_pairs={{0,4},{1,5},{2,6},{3,7},{4,0},{5,1},{6,2},{7,3},{8,12},{9,13},{10,... | collective-permute-start | bytes 98312 | tf_op jit(solution)/shard_map/ppermute | solution.py:323
  9.3 0.0 copy-start.3
  9.3 0.0 copy-start
  9.3 1.2 %fusion.1 = (f32[64,2,2,2,128]{4,3,2,1,0:T(2,128)S(1)}, f32[64,2,2,2,128]{4,3,2,1,0:T(2,128)S(1)}) fusion(f32[128,2,2,2,128]{4,3,2,1,0:T(2,128)} %bitcast.15), kind=kLoop, calls=%fused_computation.7 | loop fusion | bytes 1048576 | tf_op jit(solution)/shard_map/slice | solution.py:327
  10.5 1.5 %collective-permute-start.8 = (f32[512,128]{1,0:T(8,128)S(1)}, f32[512,128]{1,0:T(8,128)S(1)}, u32[]{:S(2)}, u32[]{:S(2)}) collective-permute-start(f32[512,128]{1,0:T(8,128)S(1)} %bitcast.19), channel_id=1, source_target_pairs={{1,0},{2,1},{3,2},{4,3},{5,4},{6,5},{7,6},{8,7},{9,8},{10,9},{11,1... | collective-permute-start | bytes 786440 | tf_op jit(solution)/shard_map/ppermute | solution.py:351
  12.6 0.0 collective-permute-done.6
  12.7 0.0 copy-done.3
  12.7 0.0 copy-start.5
  12.7 0.0 copy-start.6
  12.7 0.6 %collective-permute-start.7 = (f32[128,128]{1,0:T(8,128)S(1)}, f32[128,128]{1,0:T(8,128)S(1)}, u32[]{:S(2)}, u32[]{:S(2)}) collective-permute-start(f32[128,128]{1,0:T(8,128)S(1)} %pad_maximum_fusion.1), channel_id=1, source_target_pairs={{0,2},{1,3},{2,0},{3,1},{4,6},{5,7},{6,4},{7,5},{8,10},{9,11},{10,... | collective-permute-start | bytes 196616 | tf_op jit(solution)/shard_map/ppermute | solution.py:323
  13.3 1.9 %collective-permute-start.9 = (f32[512,128]{1,0:T(8,128)S(1)}, f32[512,128]{1,0:T(8,128)S(1)}, u32[]{:S(2)}, u32[]{:S(2)}) collective-permute-start(f32[512,128]{1,0:T(8,128)S(1)} %bitcast.18), channel_id=1, source_target_pairs={{1,0},{2,1},{3,2},{4,3},{5,4},{6,5},{7,6},{8,7},{9,8},{10,9},{11,1... | collective-permute-start | bytes 786440 | tf_op jit(solution)/shard_map/ppermute | solution.py:358
  15.1 0.0 copy-done.5
  15.1 0.0 copy-done.6
  15.1 0.1 pad_add_fusion.scalars_ref
  15.2 0.0 copy-done
  15.2 0.0 copy-start.1
  15.2 1.2 %copy-done.1 = f32[16,128,128]{2,1,0:T(8,128)S(1)} copy-done((f32[16,128,128]{2,1,0:T(8,128)S(1)}, f32[16,128,128]{2,1,0:T(8,128)}, u32[]{:S(2)}) %copy-start.1) | copy-done | bytes 1048600
  16.4 0.0 copy-start.2
  16.4 1.1 %copy-done.2 = f32[12,128,128]{2,1,0:T(8,128)S(1)} copy-done((f32[12,128,128]{2,1,0:T(8,128)S(1)}, f32[12,128,128]{2,1,0:T(8,128)}, u32[]{:S(2)}) %copy-start.2) | copy-done | bytes 786456
  17.6 0.6 %shard_map.86 = (f32[8,128,128]{2,1,0:T(8,128)S(1)}, f32[16,128,128]{2,1,0:T(8,128)S(1)}, bf16[8,256,256]{2,1,0:T(8,128)(2,1)S(1)}, bf16[8,256,256]{2,1,0:T(8,128)(2,1)S(1)}) custom-call(f32[1024,128]{1,0:T(8,128)S(1)} %bitcast.16, f32[16,128,128]{2,1,0:T(8,128)S(1)} %copy-done.1, f32[12,128,128]{2,1,0:T(8,128)S(1)} %copy-done.2), custom_call_target="tpu_custom_call" | custom-call | bytes 6291456 | tf_op jit(solution)/shard_map/pallas_call | solution.py:257
  18.1 0.9 %collective-permute-done.7 = f32[128,128]{1,0:T(8,128)S(1)} collective-permute-done((f32[128,128]{1,0:T(8,128)S(1)}, f32[128,128]{1,0:T(8,128)S(1)}, u32[]{:S(2)}, u32[]{:S(2)}) %collective-permute-start.7) | collective-permute-done | bytes 65568 | tf_op jit(solution)/shard_map/ppermute | solution.py:323
  19.1 0.1 collective-permute-start.10
  19.2 1.3 %collective-permute-done.10.far_ref = f32[256,128]{1,0:T(8,128)S(1)} collective-permute-done((f32[256,128]{1,0:T(8,128)S(1)}, f32[256,128]{1,0:T(8,128)S(1)}, u32[]{:S(2)}, u32[]{:S(2)}) %collective-permute-start.10) | collective-permute-done | bytes 131104 | tf_op jit(solution)/shard_map/ppermute | solution.py:323
  20.5 0.0 collective-permute-done.8.low_ref
  20.5 0.0 collective-permute-done.9.high_ref
  20.5 7.9 %shard_map.87 = (f32[1024,128]{1,0:T(8,128)S(1)}, f32[1024,128]{1,0:T(8,128)S(1)}, f32[4,128,128]{2,1,0:T(8,128)S(1)}) custom-call(s32[33]{0:T(128)S(1)} %pad_add_fusion.scalars_ref, f32[8,128,128]{2,1,0:T(8,128)S(1)} %get-tuple-element.34.own_ref, f32[512,128]{1,0:T(8,128)S(1)} %collective-permute-done.8.low_ref, ...), custom_call_target="tpu_custom_call" | custom-call | tf_op jit(solution)/shard_map/pallas_call | solution.py:282
  28.4 0.3 collective-permute-start.11
  28.7 25.1 %conditional.1 = (f32[8,2,2,128]{3,2,1,0:T(2,128)S(1)}) conditional(s32[]{:T(128)} %bitcast.11, () %tuple.20, f32[4,128,128]{2,1,0:T(8,128)S(1)} %get-tuple-element.42), branch_computations={%region_0.0_spmd, %region_1.0_spmd} | conditional | flops 61440 | bytes 1818832 | solution.py:366
  28.7 2.4 %collective-permute-start = (f32[256,128]{1,0:T(8,128)S(1)}, f32[256,128]{1,0:T(8,128)S(1)}, u32[]{:S(2)}, u32[]{:S(2)}) collective-permute-start(f32[256,128]{1,0:T(8,128)S(1)} %get-tuple-element.6), channel_id=1, source_target_pairs={{0,1},{1,0},{2,3},{3,2},{4,5},{5,4},{6,7},{7,6},{8,9},{9,8},{10,11... | collective-permute-start | bytes 393224 | tf_op jit(solution)/shard_map/cond/branch_1_fun/ppermute | solution.py:323
  31.1 1.0 %collective-permute-done = f32[256,128]{1,0:T(8,128)S(1)} collective-permute-done((f32[256,128]{1,0:T(8,128)S(1)}, f32[256,128]{1,0:T(8,128)S(1)}, u32[]{:S(2)}, u32[]{:S(2)}) %collective-permute-start) | collective-permute-done | bytes 131104 | tf_op jit(solution)/shard_map/cond/branch_1_fun/ppermute | solution.py:323
  32.1 12.2 %collective-permute-start.2 = (f32[64,128]{1,0:T(8,128)S(1)}, f32[64,128]{1,0:T(8,128)S(1)}, u32[]{:S(2)}, u32[]{:S(2)}) collective-permute-start(f32[64,128]{1,0:T(8,128)S(1)} %get-tuple-element.43), channel_id=1, source_target_pairs={{0,8},{1,9},{2,10},{3,11},{4,12},{5,13},{6,14},{7,15},{8,0},{9,1},... | collective-permute-start | bytes 98312 | tf_op jit(solution)/shard_map/cond/branch_1_fun/ppermute | solution.py:332
  44.3 0.0 collective-permute-start.3
  44.3 2.0 %collective-permute-start.1 = (f32[64,128]{1,0:T(8,128)S(1)}, f32[64,128]{1,0:T(8,128)S(1)}, u32[]{:S(2)}, u32[]{:S(2)}) collective-permute-start(f32[64,128]{1,0:T(8,128)S(1)} %get-tuple-element.45), channel_id=1, source_target_pairs={{0,4},{1,5},{2,6},{3,7},{4,8},{5,9},{6,10},{7,11},{8,12},{9,13},{1... | collective-permute-start | bytes 98312 | tf_op jit(solution)/shard_map/cond/branch_1_fun/ppermute | solution.py:332
  46.3 0.2 collective-permute-done.2
  46.5 1.7 %collective-permute-done.3 = f32[64,128]{1,0:T(8,128)S(1)} collective-permute-done((f32[64,128]{1,0:T(8,128)S(1)}, f32[64,128]{1,0:T(8,128)S(1)}, u32[]{:S(2)}, u32[]{:S(2)}) %collective-permute-start.3) | collective-permute-done | bytes 32800 | tf_op jit(solution)/shard_map/cond/branch_1_fun/ppermute | solution.py:332
  48.2 1.8 %collective-permute-done.1 = f32[64,128]{1,0:T(8,128)S(1)} collective-permute-done((f32[64,128]{1,0:T(8,128)S(1)}, f32[64,128]{1,0:T(8,128)S(1)}, u32[]{:S(2)}, u32[]{:S(2)}) %collective-permute-start.1) | collective-permute-done | bytes 32800 | tf_op jit(solution)/shard_map/cond/branch_1_fun/ppermute | solution.py:332
  50.0 0.6 %collective-permute-start.4 = (f32[32,128]{1,0:T(8,128)S(1)}, f32[32,128]{1,0:T(8,128)S(1)}, u32[]{:S(2)}, u32[]{:S(2)}) collective-permute-start(f32[32,128]{1,0:T(8,128)S(1)} %slice.23), channel_id=1, source_target_pairs={{0,2},{1,3},{2,0},{3,1},{4,6},{5,7},{6,4},{7,5},{8,10},{9,11},{10,... | collective-permute-start | bytes 49160 | tf_op jit(solution)/shard_map/cond/branch_1_fun/ppermute | solution.py:323
  50.6 3.2 %collective-permute-done.4 = f32[32,128]{1,0:T(8,128)S(1)} collective-permute-done((f32[32,128]{1,0:T(8,128)S(1)}, f32[32,128]{1,0:T(8,128)S(1)}, u32[]{:S(2)}, u32[]{:S(2)}) %collective-permute-start.4) | collective-permute-done | bytes 16416 | tf_op jit(solution)/shard_map/cond/branch_1_fun/ppermute | solution.py:323
  53.8 0.0 copy-start.4
  53.8 0.0 collective-permute-done.11
  53.8 0.8 %add.18 = f32[1024,128]{1,0:T(8,128)} add(f32[1024,128]{1,0:T(8,128)S(1)} %get-tuple-element.40, f32[1024,128]{1,0:T(8,128)S(1)} %collective-permute-done.11) | non-fusion elementwise | flops 131072 | bytes 1572864 | tf_op jit(solution)/shard_map/add | solution.py:371
  54.7 0.0 copy-done.4
  (8 shorter events, 0.1 us)
Async XLA Ops:
  0.6 6.0 %collective-permute-start.5 = (f32[32,128]{1,0:T(8,128)}, f32[32,128]{1,0:T(8,128)S(1)}, u32[]{:S(2)}, u32[]{:S(2)}) collective-permute-start(f32[32,128]{1,0:T(8,128)} %bitcast.20), channel_id=1, source_target_pairs={{0,8},{1,9},{2,10},{3,11},{4,12},{5,13},{6,14},{7,15},{8,0},{9,1},... | collective-permute-start | bytes 49160 | tf_op jit(solution)/shard_map/ppermute | solution.py:323
  7.4 5.3 %collective-permute-start.6 = (f32[64,128]{1,0:T(8,128)S(1)}, f32[64,128]{1,0:T(8,128)S(1)}, u32[]{:S(2)}, u32[]{:S(2)}) collective-permute-start(f32[64,128]{1,0:T(8,128)S(1)} %pad_maximum_fusion.2), channel_id=1, source_target_pairs={{0,4},{1,5},{2,6},{3,7},{4,0},{5,1},{6,2},{7,3},{8,12},{9,13},{10,... | collective-permute-start | bytes 98312 | tf_op jit(solution)/shard_map/ppermute | solution.py:323
  9.3 3.4 %copy-start.3 = (f32[8,2,2,128]{3,2,1,0:T(2,128)S(1)}, f32[8,2,2,128]{3,2,1,0:T(2,128)}, u32[]{:S(2)}) copy-start(f32[8,2,2,128]{3,2,1,0:T(2,128)} %param.10) | copy-start | bytes 49156
  9.3 5.9 %copy-start = (f32[128,2,2,256]{3,2,1,0:T(2,128)S(1)}, f32[128,2,2,256]{3,2,1,0:T(2,128)}, u32[]{:S(2)}) copy-start(f32[128,2,2,256]{3,2,1,0:T(2,128)} %param.9) | copy-start | bytes 1572868
  10.5 10.0 %collective-permute-start.8 = (f32[512,128]{1,0:T(8,128)S(1)}, f32[512,128]{1,0:T(8,128)S(1)}, u32[]{:S(2)}, u32[]{:S(2)}) collective-permute-start(f32[512,128]{1,0:T(8,128)S(1)} %bitcast.19), channel_id=1, source_target_pairs={{1,0},{2,1},{3,2},{4,3},{5,4},{6,5},{7,6},{8,7},{9,8},{10,9},{11,1... | collective-permute-start | bytes 786440 | tf_op jit(solution)/shard_map/ppermute | solution.py:351
  12.7 2.5 %copy-start.5 = (s32[16]{0:T(128)S(1)}, s32[16]{0:T(128)}, u32[]{:S(2)}) copy-start(s32[16]{0:T(128)} %param.13) | copy-start | bytes 196
  12.7 2.4 %copy-start.6 = (s32[16]{0:T(128)S(1)}, s32[16]{0:T(128)}, u32[]{:S(2)}) copy-start(s32[16]{0:T(128)} %param.12) | copy-start | bytes 196
  12.7 6.4 %collective-permute-start.7 = (f32[128,128]{1,0:T(8,128)S(1)}, f32[128,128]{1,0:T(8,128)S(1)}, u32[]{:S(2)}, u32[]{:S(2)}) collective-permute-start(f32[128,128]{1,0:T(8,128)S(1)} %pad_maximum_fusion.1), channel_id=1, source_target_pairs={{0,2},{1,3},{2,0},{3,1},{4,6},{5,7},{6,4},{7,5},{8,10},{9,11},{10,... | collective-permute-start | bytes 196616 | tf_op jit(solution)/shard_map/ppermute | solution.py:323
  13.3 7.2 %collective-permute-start.9 = (f32[512,128]{1,0:T(8,128)S(1)}, f32[512,128]{1,0:T(8,128)S(1)}, u32[]{:S(2)}, u32[]{:S(2)}) collective-permute-start(f32[512,128]{1,0:T(8,128)S(1)} %bitcast.18), channel_id=1, source_target_pairs={{1,0},{2,1},{3,2},{4,3},{5,4},{6,5},{7,6},{8,7},{9,8},{10,9},{11,1... | collective-permute-start | bytes 786440 | tf_op jit(solution)/shard_map/ppermute | solution.py:358
  15.2 1.2 %copy-start.1 = (f32[16,128,128]{2,1,0:T(8,128)S(1)}, f32[16,128,128]{2,1,0:T(8,128)}, u32[]{:S(2)}) copy-start(f32[16,128,128]{2,1,0:T(8,128)} %patterns_ref) | copy-start | bytes 3145732
  16.4 1.1 %copy-start.2 = (f32[12,128,128]{2,1,0:T(8,128)S(1)}, f32[12,128,128]{2,1,0:T(8,128)}, u32[]{:S(2)}) copy-start(f32[12,128,128]{2,1,0:T(8,128)} %constant.7.clone.factors_ref) | copy-start | bytes 2359300
  19.1 1.4 %collective-permute-start.10 = (f32[256,128]{1,0:T(8,128)S(1)}, f32[256,128]{1,0:T(8,128)S(1)}, u32[]{:S(2)}, u32[]{:S(2)}) collective-permute-start(f32[256,128]{1,0:T(8,128)S(1)} %pad_maximum_fusion.near_ref), channel_id=1, source_target_pairs={{0,1},{1,0},{2,3},{3,2},{4,5},{5,4},{6,7},{7,6},{8,9},{9,8},{10,11... | collective-permute-start | bytes 393224 | tf_op jit(solution)/shard_map/ppermute | solution.py:323
  28.4 25.4 %collective-permute-start.11 = (f32[1024,128]{1,0:T(8,128)S(1)}, f32[1024,128]{1,0:T(8,128)S(1)}, u32[]{:S(2)}, u32[]{:S(2)}) collective-permute-start(f32[1024,128]{1,0:T(8,128)S(1)} %get-tuple-element.41), channel_id=1, source_target_pairs={{0,1},{1,2},{2,3},{3,4},{4,5},{5,6},{6,7},{7,8},{8,9},{9,10},{10,1... | collective-permute-start | bytes 1572872 | tf_op jit(solution)/shard_map/ppermute | solution.py:365
  28.7 3.3 %collective-permute-start = (f32[256,128]{1,0:T(8,128)S(1)}, f32[256,128]{1,0:T(8,128)S(1)}, u32[]{:S(2)}, u32[]{:S(2)}) collective-permute-start(f32[256,128]{1,0:T(8,128)S(1)} %get-tuple-element.6), channel_id=1, source_target_pairs={{0,1},{1,0},{2,3},{3,2},{4,5},{5,4},{6,7},{7,6},{8,9},{9,8},{10,11... | collective-permute-start | bytes 393224 | tf_op jit(solution)/shard_map/cond/branch_1_fun/ppermute | solution.py:323
  32.1 14.4 %collective-permute-start.2 = (f32[64,128]{1,0:T(8,128)S(1)}, f32[64,128]{1,0:T(8,128)S(1)}, u32[]{:S(2)}, u32[]{:S(2)}) collective-permute-start(f32[64,128]{1,0:T(8,128)S(1)} %get-tuple-element.43), channel_id=1, source_target_pairs={{0,8},{1,9},{2,10},{3,11},{4,12},{5,13},{6,14},{7,15},{8,0},{9,1},... | collective-permute-start | bytes 98312 | tf_op jit(solution)/shard_map/cond/branch_1_fun/ppermute | solution.py:332
  44.3 3.9 %collective-permute-start.3 = (f32[64,128]{1,0:T(8,128)S(1)}, f32[64,128]{1,0:T(8,128)S(1)}, u32[]{:S(2)}, u32[]{:S(2)}) collective-permute-start(f32[64,128]{1,0:T(8,128)S(1)} %get-tuple-element.44), channel_id=1, source_target_pairs={{0,12},{1,13},{2,14},{3,15},{4,0},{5,1},{6,2},{7,3},{8,4},{9,5},{1... | collective-permute-start | bytes 98312 | tf_op jit(solution)/shard_map/cond/branch_1_fun/ppermute | solution.py:332
  44.3 5.7 %collective-permute-start.1 = (f32[64,128]{1,0:T(8,128)S(1)}, f32[64,128]{1,0:T(8,128)S(1)}, u32[]{:S(2)}, u32[]{:S(2)}) collective-permute-start(f32[64,128]{1,0:T(8,128)S(1)} %get-tuple-element.45), channel_id=1, source_target_pairs={{0,4},{1,5},{2,6},{3,7},{4,8},{5,9},{6,10},{7,11},{8,12},{9,13},{1... | collective-permute-start | bytes 98312 | tf_op jit(solution)/shard_map/cond/branch_1_fun/ppermute | solution.py:332
  50.0 3.8 %collective-permute-start.4 = (f32[32,128]{1,0:T(8,128)S(1)}, f32[32,128]{1,0:T(8,128)S(1)}, u32[]{:S(2)}, u32[]{:S(2)}) collective-permute-start(f32[32,128]{1,0:T(8,128)S(1)} %slice.23), channel_id=1, source_target_pairs={{0,2},{1,3},{2,0},{3,1},{4,6},{5,7},{6,4},{7,5},{8,10},{9,11},{10,... | collective-permute-start | bytes 49160 | tf_op jit(solution)/shard_map/cond/branch_1_fun/ppermute | solution.py:323
  53.8 0.9 %copy-start.4 = (f32[8,2,2,128]{3,2,1,0:T(2,128)}, f32[8,2,2,128]{3,2,1,0:T(2,128)S(1)}, u32[]{:S(2)}) copy-start(f32[8,2,2,128]{3,2,1,0:T(2,128)S(1)} %get-tuple-element.48) | copy-start | bytes 49156
where the time goes:
time: 54.8 us; the launch traced here: 54.7 us
  starting transfers between devices  27.4 us (50%)
  waiting for transfers between devices  12.1 us (22%)
  Pallas kernels  8.48 us (15%)
  local copies, waits for them, and re-layouts  3.62 us (7%)
  other arithmetic  1.69 us (3%)
  between operations  1.36 us (2%)
    ppermute x3, starting transfers between devices, places_on(): lax.ppermute(value, 'tile', [(i, i // GROUP_DEV * GROUP_DEV + (i + distan...  14.2 us
    ppermute x6, starting transfers between devices, partner(): lax.ppermute(value, 'tile', [(i, i ^ bits) for i in range(lax.axis_size('...  9.62 us
    ppermute x6, waiting for transfers between devices, partner(): lax.ppermute(value, 'tile', [(i, i ^ bits) for i in range(lax.axis_size('...  8.39 us
    pallas_call x1, Pallas kernels, terms(): pl.pallas_call(kernel, out_shape=(jax.ShapeDtypeStruct((planes.shape[1] *...  7.89 us
    ppermute x3, waiting for transfers between devices, places_on(): lax.ppermute(value, 'tile', [(i, i // GROUP_DEV * GROUP_DEV + (i + distan...  3.69 us
    unnamed x14, local copies, waits for them, and re-layouts  2.38 us
    ppermute x1, starting transfers between devices, shards(): high = lax.ppermute(high, 'tile', down)  1.85 us
    ppermute x1, starting transfers between devices, shards(): low = lax.ppermute(low, 'tile', down)  1.47 us
  transfers between devices with their start and end apart: 12, of which 8 were waited for; matrix products, arithmetic and copies ran while one was open for 2% of the time, Pallas kernels for 1%

commit v1 on v0

--- a/solution.py
+++ b/solution.py
@@ -348,16 +348,16 @@
     low, high = halved(own)
     scalars = jnp.concatenate([row_offsets, col_offsets, counts])
 
+    low, high, mine = lax.optimization_barrier((low, high, flat(probe_field)))
     low = lax.ppermute(low, "tile", down)
-    mine = flat(probe_field)
     quarter = mine
     for bits in (8, 4):
         quarter = jnp.concatenate([quarter, partner(quarter, bits)], axis=0)
-    high, quarter, patterns, own = lax.optimization_barrier((high, quarter, patterns, own))
+    planes, patterns, *mats = prepared(own, patterns)
+    low, high, quarter, planes, patterns, scalars, *mats = lax.optimization_barrier(
+        (low, high, quarter, planes, patterns, scalars, *mats))
     near = jnp.concatenate([quarter, partner(quarter, 2)], axis=0)
     high = lax.ppermute(high, "tile", down)
-    planes, patterns, *mats = prepared(own, patterns)
-    near, planes, patterns, scalars, *mats = lax.optimization_barrier((near, planes, patterns, scalars, *mats))
     far = partner(near, 1)
 
     own_grad, back, probe_grad = terms(scalars, planes, low, high, near, far, patterns, mats)

time: 54.8 us -> 53.5 us (0.976)
  waiting for transfers between devices: 12.1 us -> 14.8 us
  starting transfers between devices: 27.4 us -> 25.5 us
  Pallas kernels: 8.48 us -> 7.06 us
  other arithmetic: 1.69 us -> 0.96 us
    ppermute x3, starting transfers between devices: 14.2 us -> 9.9 us  [places_on(): lax.ppermute(value, 'tile', [(i, i // GROUP_DEV * GROUP_DEV + (i + distan...]
    ppermute x6, starting transfers between devices: 9.62 us -> 12 us  [partner(): lax.ppermute(value, 'tile', [(i, i ^ bits) for i in range(lax.axis_size('...]
    ppermute x3, waiting for transfers between devices: 3.69 us -> 5.71 us  [places_on(): lax.ppermute(value, 'tile', [(i, i // GROUP_DEV * GROUP_DEV + (i + distan...]
    pallas_call x1, Pallas kernels: 7.89 us -> 6.46 us  [terms(): pl.pallas_call(kernel, out_shape=(jax.ShapeDtypeStruct((planes.shape[1] *...]
    concatenate x2, other arithmetic: 0.73 us -> 0.01 us  [shards(): quarter = jnp.concatenate([quarter, partner(quarter, bits)], axis=0)]
    ppermute x6, waiting for transfers between devices: 8.39 us -> 9.08 us  [partner(): lax.ppermute(value, 'tile', [(i, i ^ bits) for i in range(lax.axis_size('...]
    unnamed x14 -> x15, local copies, waits for them, and re-layouts: 2.38 us -> 2.39 us
  transfers between devices with their start and end apart: 12 -> 12, of which waited for: 8 -> 7; matrix products, arithmetic and copies ran while one was open for 2% -> 0% of each run, Pallas kernels for 1% -> 1%
where the time goes in v1:
time: 53.5 us
  starting transfers between devices  25.5 us (48%)
  waiting for transfers between devices  14.8 us (28%)
  Pallas kernels  7.06 us (13%)
  local copies, waits for them, and re-layouts  3.63 us (7%)
  between operations  1.39 us (3%)
  other arithmetic  0.96 us (2%)
    ppermute x6, starting transfers between devices, partner(): lax.ppermute(value, 'tile', [(i, i ^ bits) for i in range(lax.axis_size('...  12 us
    ppermute x3, starting transfers between devices, places_on(): lax.ppermute(value, 'tile', [(i, i // GROUP_DEV * GROUP_DEV + (i + distan...  9.9 us
    ppermute x6, waiting for transfers between devices, partner(): lax.ppermute(value, 'tile', [(i, i ^ bits) for i in range(lax.axis_size('...  9.08 us
    pallas_call x1, Pallas kernels, terms(): pl.pallas_call(kernel, out_shape=(jax.ShapeDtypeStruct((planes.shape[1] *...  6.46 us
    ppermute x3, waiting for transfers between devices, places_on(): lax.ppermute(value, 'tile', [(i, i // GROUP_DEV * GROUP_DEV + (i + distan...  5.71 us
    unnamed x15, local copies, waits for them, and re-layouts  2.39 us
    ppermute x1, starting transfers between devices, shards(): high = lax.ppermute(high, 'tile', down)  2.12 us
    ppermute x1, starting transfers between devices, shards(): low = lax.ppermute(low, 'tile', down)  1.45 us
  transfers between devices with their start and end apart: 12, of which 7 were waited for; matrix products, arithmetic and copies ran while one was open for 0% of the time, Pallas kernels for 1%

profile of v1, /device:TPU:0, one launch (start us, length us, event | category | flops | bytes accessed | tf_op | source)
XLA Modules:
  0.0 53.5 jit_solution(12099824176842107232)
XLA Ops:
  0.6 0.0 copy-start.3
  0.6 0.0 copy-start
  0.6 1.2 %fusion.1 = (f32[64,2,2,2,128]{4,3,2,1,0:T(2,128)S(1)}, f32[64,2,2,2,128]{4,3,2,1,0:T(2,128)S(1)}) fusion(f32[128,2,2,2,128]{4,3,2,1,0:T(2,128)} %bitcast.15), kind=kLoop, calls=%fused_computation.8 | loop fusion | bytes 1048576 | tf_op jit(solution)/shard_map/slice | solution.py:327
  1.9 0.0 copy-done.3
  1.9 4.1 %collective-permute-start.6 = (f32[32,128]{1,0:T(8,128)S(1)}, f32[32,128]{1,0:T(8,128)S(1)}, u32[]{:S(2)}, u32[]{:S(2)}) collective-permute-start(f32[32,128]{1,0:T(8,128)S(1)} %bitcast.20), channel_id=1, source_target_pairs={{0,8},{1,9},{2,10},{3,11},{4,12},{5,13},{6,14},{7,15},{8,0},{9,1},... | collective-permute-start | bytes 49160 | tf_op jit(solution)/shard_map/ppermute | solution.py:323
  6.0 1.4 %collective-permute-start.5 = (f32[512,128]{1,0:T(8,128)S(1)}, f32[512,128]{1,0:T(8,128)S(1)}, u32[]{:S(2)}, u32[]{:S(2)}) collective-permute-start(f32[512,128]{1,0:T(8,128)S(1)} %bitcast.19), channel_id=1, source_target_pairs={{1,0},{2,1},{3,2},{4,3},{5,4},{6,5},{7,6},{8,7},{9,8},{10,9},{11,1... | collective-permute-start | bytes 786440 | tf_op jit(solution)/shard_map/ppermute | solution.py:352
  8.1 0.0 copy-start.5
  8.1 0.0 copy-start.6
  8.1 0.0 collective-permute-done.6
  8.1 1.5 %collective-permute-start.7 = (f32[64,128]{1,0:T(8,128)S(1)}, f32[64,128]{1,0:T(8,128)S(1)}, u32[]{:S(2)}, u32[]{:S(2)}) collective-permute-start(f32[64,128]{1,0:T(8,128)S(1)} %pad_maximum_fusion.1), channel_id=1, source_target_pairs={{0,4},{1,5},{2,6},{3,7},{4,0},{5,1},{6,2},{7,3},{8,12},{9,13},{10,... | collective-permute-start | bytes 98312 | tf_op jit(solution)/shard_map/ppermute | solution.py:323
  9.6 0.0 copy-done.5
  9.6 0.0 copy-done.6
  9.6 0.1 pad_add_fusion.scalars_ref
  9.7 0.0 copy-done
  9.7 0.0 copy-start.1
  9.7 1.2 %copy-done.1 = f32[16,128,128]{2,1,0:T(8,128)S(1)} copy-done((f32[16,128,128]{2,1,0:T(8,128)S(1)}, f32[16,128,128]{2,1,0:T(8,128)}, u32[]{:S(2)}) %copy-start.1) | copy-done | bytes 1048600
  10.9 0.0 copy-start.2
  10.9 1.1 %copy-done.2 = f32[12,128,128]{2,1,0:T(8,128)S(1)} copy-done((f32[12,128,128]{2,1,0:T(8,128)S(1)}, f32[12,128,128]{2,1,0:T(8,128)}, u32[]{:S(2)}) %copy-start.2) | copy-done | bytes 786456
  12.1 0.6 %shard_map.86 = (f32[8,128,128]{2,1,0:T(8,128)S(1)}, f32[16,128,128]{2,1,0:T(8,128)S(1)}, bf16[8,256,256]{2,1,0:T(8,128)(2,1)S(1)}, bf16[8,256,256]{2,1,0:T(8,128)(2,1)S(1)}) custom-call(f32[1024,128]{1,0:T(8,128)S(1)} %bitcast.16, f32[16,128,128]{2,1,0:T(8,128)S(1)} %copy-done.1, f32[12,128,128]{2,1,0:T(8,128)S(1)} %copy-done.2), custom_call_target="tpu_custom_call" | custom-call | bytes 6291456 | tf_op jit(solution)/shard_map/pallas_call | solution.py:257
  12.6 0.5 collective-permute-done.7
  13.2 0.0 collective-permute-done.5.low_ref
  13.2 1.1 %collective-permute-start.9 = (f32[128,128]{1,0:T(8,128)S(1)}, f32[128,128]{1,0:T(8,128)S(1)}, u32[]{:S(2)}, u32[]{:S(2)}) collective-permute-start(f32[128,128]{1,0:T(8,128)S(1)} %pad_maximum_fusion), channel_id=1, source_target_pairs={{0,2},{1,3},{2,0},{3,1},{4,6},{5,7},{6,4},{7,5},{8,10},{9,11},{10,... | collective-permute-start | bytes 196616 | tf_op jit(solution)/shard_map/ppermute | solution.py:323
  14.2 2.1 %collective-permute-start.8 = (f32[512,128]{1,0:T(8,128)S(1)}, f32[512,128]{1,0:T(8,128)S(1)}, u32[]{:S(2)}, u32[]{:S(2)}) collective-permute-start(f32[512,128]{1,0:T(8,128)S(1)} %bitcast.18), channel_id=1, source_target_pairs={{1,0},{2,1},{3,2},{4,3},{5,4},{6,5},{7,6},{8,7},{9,8},{10,9},{11,1... | collective-permute-start | bytes 786440 | tf_op jit(solution)/shard_map/ppermute | solution.py:360
  16.4 2.5 %collective-permute-done.9 = f32[128,128]{1,0:T(8,128)S(1)} collective-permute-done((f32[128,128]{1,0:T(8,128)S(1)}, f32[128,128]{1,0:T(8,128)S(1)}, u32[]{:S(2)}, u32[]{:S(2)}) %collective-permute-start.9) | collective-permute-done | bytes 65568 | tf_op jit(solution)/shard_map/ppermute | solution.py:323
  18.9 0.0 collective-permute-start.10
  18.9 1.3 %collective-permute-done.10.far_ref = f32[256,128]{1,0:T(8,128)S(1)} collective-permute-done((f32[256,128]{1,0:T(8,128)S(1)}, f32[256,128]{1,0:T(8,128)S(1)}, u32[]{:S(2)}, u32[]{:S(2)}) %collective-permute-start.10) | collective-permute-done | bytes 131104 | tf_op jit(solution)/shard_map/ppermute | solution.py:323
  20.2 0.0 collective-permute-done.8.high_ref
  20.2 6.5 %shard_map.87 = (f32[1024,128]{1,0:T(8,128)S(1)}, f32[1024,128]{1,0:T(8,128)S(1)}, f32[4,128,128]{2,1,0:T(8,128)S(1)}) custom-call(s32[33]{0:T(128)S(1)} %pad_add_fusion.scalars_ref, f32[8,128,128]{2,1,0:T(8,128)S(1)} %get-tuple-element.35.own_ref, f32[512,128]{1,0:T(8,128)S(1)} %collective-permute-done.5.low_ref, ...), custom_call_target="tpu_custom_call" | custom-call | tf_op jit(solution)/shard_map/pallas_call | solution.py:282
  26.7 0.1 collective-permute-start.11
  26.8 25.8 %conditional.1 = (f32[8,2,2,128]{3,2,1,0:T(2,128)S(1)}) conditional(s32[]{:T(128)} %bitcast.11, () %tuple.20, f32[4,128,128]{2,1,0:T(8,128)S(1)} %get-tuple-element.44), branch_computations={%region_0.0_spmd, %region_1.0_spmd} | conditional | flops 61440 | bytes 1818832 | solution.py:366
  26.8 5.3 %collective-permute-start = (f32[256,128]{1,0:T(8,128)S(1)}, f32[256,128]{1,0:T(8,128)S(1)}, u32[]{:S(2)}, u32[]{:S(2)}) collective-permute-start(f32[256,128]{1,0:T(8,128)S(1)} %get-tuple-element.6), channel_id=1, source_target_pairs={{0,1},{1,0},{2,3},{3,2},{4,5},{5,4},{6,7},{7,6},{8,9},{9,8},{10,11... | collective-permute-start | bytes 393224 | tf_op jit(solution)/shard_map/cond/branch_1_fun/ppermute | solution.py:323
  32.2 1.0 %collective-permute-done = f32[256,128]{1,0:T(8,128)S(1)} collective-permute-done((f32[256,128]{1,0:T(8,128)S(1)}, f32[256,128]{1,0:T(8,128)S(1)}, u32[]{:S(2)}, u32[]{:S(2)}) %collective-permute-start) | collective-permute-done | bytes 131104 | tf_op jit(solution)/shard_map/cond/branch_1_fun/ppermute | solution.py:323
  33.2 2.0 %collective-permute-start.2 = (f32[64,128]{1,0:T(8,128)S(1)}, f32[64,128]{1,0:T(8,128)S(1)}, u32[]{:S(2)}, u32[]{:S(2)}) collective-permute-start(f32[64,128]{1,0:T(8,128)S(1)} %get-tuple-element.45), channel_id=1, source_target_pairs={{0,8},{1,9},{2,10},{3,11},{4,12},{5,13},{6,14},{7,15},{8,0},{9,1},... | collective-permute-start | bytes 98312 | tf_op jit(solution)/shard_map/cond/branch_1_fun/ppermute | solution.py:332
  35.2 7.8 %collective-permute-start.3 = (f32[64,128]{1,0:T(8,128)S(1)}, f32[64,128]{1,0:T(8,128)S(1)}, u32[]{:S(2)}, u32[]{:S(2)}) collective-permute-start(f32[64,128]{1,0:T(8,128)S(1)} %get-tuple-element.46), channel_id=1, source_target_pairs={{0,12},{1,13},{2,14},{3,15},{4,0},{5,1},{6,2},{7,3},{8,4},{9,5},{1... | collective-permute-start | bytes 98312 | tf_op jit(solution)/shard_map/cond/branch_1_fun/ppermute | solution.py:332
  43.1 0.0 collective-permute-start.1
  43.1 0.0 collective-permute-done.2
  43.1 1.6 %collective-permute-done.3 = f32[64,128]{1,0:T(8,128)S(1)} collective-permute-done((f32[64,128]{1,0:T(8,128)S(1)}, f32[64,128]{1,0:T(8,128)S(1)}, u32[]{:S(2)}, u32[]{:S(2)}) %collective-permute-start.3) | collective-permute-done | bytes 32800 | tf_op jit(solution)/shard_map/cond/branch_1_fun/ppermute | solution.py:332
  44.7 4.1 %collective-permute-done.1 = f32[64,128]{1,0:T(8,128)S(1)} collective-permute-done((f32[64,128]{1,0:T(8,128)S(1)}, f32[64,128]{1,0:T(8,128)S(1)}, u32[]{:S(2)}, u32[]{:S(2)}) %collective-permute-start.1) | collective-permute-done | bytes 32800 | tf_op jit(solution)/shard_map/cond/branch_1_fun/ppermute | solution.py:332
  48.8 0.1 collective-permute-start.4
  48.9 3.7 %collective-permute-done.4 = f32[32,128]{1,0:T(8,128)S(1)} collective-permute-done((f32[32,128]{1,0:T(8,128)S(1)}, f32[32,128]{1,0:T(8,128)S(1)}, u32[]{:S(2)}, u32[]{:S(2)}) %collective-permute-start.4) | collective-permute-done | bytes 16416 | tf_op jit(solution)/shard_map/cond/branch_1_fun/ppermute | solution.py:323
  52.6 0.0 copy-start.4
  52.6 0.0 collective-permute-done.11
  52.6 0.8 %add.18 = f32[1024,128]{1,0:T(8,128)} add(f32[1024,128]{1,0:T(8,128)S(1)} %get-tuple-element.42, f32[1024,128]{1,0:T(8,128)S(1)} %collective-permute-done.11) | non-fusion elementwise | flops 131072 | bytes 1572864 | tf_op jit(solution)/shard_map/add | solution.py:371
  53.5 0.0 copy-done.4
  (10 shorter events, 0.1 us)
Async XLA Ops:
  0.6 1.2 %copy-start.3 = (f32[8,2,2,128]{3,2,1,0:T(2,128)S(1)}, f32[8,2,2,128]{3,2,1,0:T(2,128)}, u32[]{:S(2)}) copy-start(f32[8,2,2,128]{3,2,1,0:T(2,128)} %param.10) | copy-start | bytes 49156
  0.6 9.1 %copy-start = (f32[128,2,2,256]{3,2,1,0:T(2,128)S(1)}, f32[128,2,2,256]{3,2,1,0:T(2,128)}, u32[]{:S(2)}) copy-start(f32[128,2,2,256]{3,2,1,0:T(2,128)} %param.9) | copy-start | bytes 1572868
  1.9 6.2 %collective-permute-start.6 = (f32[32,128]{1,0:T(8,128)S(1)}, f32[32,128]{1,0:T(8,128)S(1)}, u32[]{:S(2)}, u32[]{:S(2)}) collective-permute-start(f32[32,128]{1,0:T(8,128)S(1)} %bitcast.20), channel_id=1, source_target_pairs={{0,8},{1,9},{2,10},{3,11},{4,12},{5,13},{6,14},{7,15},{8,0},{9,1},... | collective-permute-start | bytes 49160 | tf_op jit(solution)/shard_map/ppermute | solution.py:323
  6.0 7.2 %collective-permute-start.5 = (f32[512,128]{1,0:T(8,128)S(1)}, f32[512,128]{1,0:T(8,128)S(1)}, u32[]{:S(2)}, u32[]{:S(2)}) collective-permute-start(f32[512,128]{1,0:T(8,128)S(1)} %bitcast.19), channel_id=1, source_target_pairs={{1,0},{2,1},{3,2},{4,3},{5,4},{6,5},{7,6},{8,7},{9,8},{10,9},{11,1... | collective-permute-start | bytes 786440 | tf_op jit(solution)/shard_map/ppermute | solution.py:352
  8.1 1.5 %copy-start.5 = (s32[16]{0:T(128)S(1)}, s32[16]{0:T(128)}, u32[]{:S(2)}) copy-start(s32[16]{0:T(128)} %param.13) | copy-start | bytes 196
  8.1 1.5 %copy-start.6 = (s32[16]{0:T(128)S(1)}, s32[16]{0:T(128)}, u32[]{:S(2)}) copy-start(s32[16]{0:T(128)} %param.12) | copy-start | bytes 196
  8.1 5.0 %collective-permute-start.7 = (f32[64,128]{1,0:T(8,128)S(1)}, f32[64,128]{1,0:T(8,128)S(1)}, u32[]{:S(2)}, u32[]{:S(2)}) collective-permute-start(f32[64,128]{1,0:T(8,128)S(1)} %pad_maximum_fusion.1), channel_id=1, source_target_pairs={{0,4},{1,5},{2,6},{3,7},{4,0},{5,1},{6,2},{7,3},{8,12},{9,13},{10,... | collective-permute-start | bytes 98312 | tf_op jit(solution)/shard_map/ppermute | solution.py:323
  9.7 1.2 %copy-start.1 = (f32[16,128,128]{2,1,0:T(8,128)S(1)}, f32[16,128,128]{2,1,0:T(8,128)}, u32[]{:S(2)}) copy-start(f32[16,128,128]{2,1,0:T(8,128)} %patterns_ref.1) | copy-start | bytes 3145732
  10.9 1.1 %copy-start.2 = (f32[12,128,128]{2,1,0:T(8,128)S(1)}, f32[12,128,128]{2,1,0:T(8,128)}, u32[]{:S(2)}) copy-start(f32[12,128,128]{2,1,0:T(8,128)} %constant.7.clone.factors_ref) | copy-start | bytes 2359300
  13.2 5.7 %collective-permute-start.9 = (f32[128,128]{1,0:T(8,128)S(1)}, f32[128,128]{1,0:T(8,128)S(1)}, u32[]{:S(2)}, u32[]{:S(2)}) collective-permute-start(f32[128,128]{1,0:T(8,128)S(1)} %pad_maximum_fusion), channel_id=1, source_target_pairs={{0,2},{1,3},{2,0},{3,1},{4,6},{5,7},{6,4},{7,5},{8,10},{9,11},{10,... | collective-permute-start | bytes 196616 | tf_op jit(solution)/shard_map/ppermute | solution.py:323
  14.2 6.0 %collective-permute-start.8 = (f32[512,128]{1,0:T(8,128)S(1)}, f32[512,128]{1,0:T(8,128)S(1)}, u32[]{:S(2)}, u32[]{:S(2)}) collective-permute-start(f32[512,128]{1,0:T(8,128)S(1)} %bitcast.18), channel_id=1, source_target_pairs={{1,0},{2,1},{3,2},{4,3},{5,4},{6,5},{7,6},{8,7},{9,8},{10,9},{11,1... | collective-permute-start | bytes 786440 | tf_op jit(solution)/shard_map/ppermute | solution.py:360
  18.9 1.3 %collective-permute-start.10 = (f32[256,128]{1,0:T(8,128)S(1)}, f32[256,128]{1,0:T(8,128)S(1)}, u32[]{:S(2)}, u32[]{:S(2)}) collective-permute-start(f32[256,128]{1,0:T(8,128)S(1)} %constant_dynamic-update-slice_fusion.near_ref), channel_id=1, source_target_pairs={{0,1},{1,0},{2,3},{3,2},{4,5},{5,4},{6,7},{7,6},{8,9},{9,8},{10,11... | collective-permute-start | bytes 393224 | tf_op jit(solution)/shard_map/ppermute | solution.py:323
  26.7 25.9 %collective-permute-start.11 = (f32[1024,128]{1,0:T(8,128)S(1)}, f32[1024,128]{1,0:T(8,128)S(1)}, u32[]{:S(2)}, u32[]{:S(2)}) collective-permute-start(f32[1024,128]{1,0:T(8,128)S(1)} %get-tuple-element.43), channel_id=1, source_target_pairs={{0,1},{1,2},{2,3},{3,4},{4,5},{5,6},{6,7},{7,8},{8,9},{9,10},{10,1... | collective-permute-start | bytes 1572872 | tf_op jit(solution)/shard_map/ppermute | solution.py:365
  26.8 6.3 %collective-permute-start = (f32[256,128]{1,0:T(8,128)S(1)}, f32[256,128]{1,0:T(8,128)S(1)}, u32[]{:S(2)}, u32[]{:S(2)}) collective-permute-start(f32[256,128]{1,0:T(8,128)S(1)} %get-tuple-element.6), channel_id=1, source_target_pairs={{0,1},{1,0},{2,3},{3,2},{4,5},{5,4},{6,7},{7,6},{8,9},{9,8},{10,11... | collective-permute-start | bytes 393224 | tf_op jit(solution)/shard_map/cond/branch_1_fun/ppermute | solution.py:323
  33.2 9.9 %collective-permute-start.2 = (f32[64,128]{1,0:T(8,128)S(1)}, f32[64,128]{1,0:T(8,128)S(1)}, u32[]{:S(2)}, u32[]{:S(2)}) collective-permute-start(f32[64,128]{1,0:T(8,128)S(1)} %get-tuple-element.45), channel_id=1, source_target_pairs={{0,8},{1,9},{2,10},{3,11},{4,12},{5,13},{6,14},{7,15},{8,0},{9,1},... | collective-permute-start | bytes 98312 | tf_op jit(solution)/shard_map/cond/branch_1_fun/ppermute | solution.py:332
  35.2 9.4 %collective-permute-start.3 = (f32[64,128]{1,0:T(8,128)S(1)}, f32[64,128]{1,0:T(8,128)S(1)}, u32[]{:S(2)}, u32[]{:S(2)}) collective-permute-start(f32[64,128]{1,0:T(8,128)S(1)} %get-tuple-element.46), channel_id=1, source_target_pairs={{0,12},{1,13},{2,14},{3,15},{4,0},{5,1},{6,2},{7,3},{8,4},{9,5},{1... | collective-permute-start | bytes 98312 | tf_op jit(solution)/shard_map/cond/branch_1_fun/ppermute | solution.py:332
  43.1 5.7 %collective-permute-start.1 = (f32[64,128]{1,0:T(8,128)S(1)}, f32[64,128]{1,0:T(8,128)S(1)}, u32[]{:S(2)}, u32[]{:S(2)}) collective-permute-start(f32[64,128]{1,0:T(8,128)S(1)} %get-tuple-element.47), channel_id=1, source_target_pairs={{0,4},{1,5},{2,6},{3,7},{4,8},{5,9},{6,10},{7,11},{8,12},{9,13},{1... | collective-permute-start | bytes 98312 | tf_op jit(solution)/shard_map/cond/branch_1_fun/ppermute | solution.py:332
  48.8 3.8 %collective-permute-start.4 = (f32[32,128]{1,0:T(8,128)S(1)}, f32[32,128]{1,0:T(8,128)S(1)}, u32[]{:S(2)}, u32[]{:S(2)}) collective-permute-start(f32[32,128]{1,0:T(8,128)S(1)} %slice.23), channel_id=1, source_target_pairs={{0,2},{1,3},{2,0},{3,1},{4,6},{5,7},{6,4},{7,5},{8,10},{9,11},{10,... | collective-permute-start | bytes 49160 | tf_op jit(solution)/shard_map/cond/branch_1_fun/ppermute | solution.py:323
  52.6 0.9 %copy-start.4 = (f32[8,2,2,128]{3,2,1,0:T(2,128)}, f32[8,2,2,128]{3,2,1,0:T(2,128)S(1)}, u32[]{:S(2)}) copy-start(f32[8,2,2,128]{3,2,1,0:T(2,128)S(1)} %get-tuple-element.50) | copy-start | bytes 49156
